TPU v7x, 128 devices: a whole 4x4x4 slice. The times are simulated.
128 devices in a mesh: depth: 2 (over core), row: 16 (over x, z), col: 4 (over y).
Axes of the slice: x: 4, y: 4, z: 4, core: 2. Of those that a mesh axis runs over, the one named last changes fastest.
Arguments:
- layer_input: bfloat16 [1024, 8192], P(('depth', 'row'), 'col'), may hold values from -6 to 6
- w_in: bfloat16 [8192, 24576], P('col', 'row'), may hold values from -0.0625 to 0.0625
- w_out: bfloat16 [24576, 8192], P('row', 'col'), may hold values from -0.0390625 to 0.0390625
- output_grad: bfloat16 [1024, 8192], P(('depth', 'row'), 'col'), may hold values from -1.5 to 1.5
Outputs:
- block_output: bfloat16 [1024, 8192], P(('depth', 'row'), 'col')
- input_grad: bfloat16 [1024, 8192], P(('depth', 'row'), 'col')
- w_in_grad: bfloat16 [8192, 24576], P('col', 'row')
- w_out_grad: bfloat16 [24576, 8192], P('row', 'col')
All inputs are finite; a program needn't handle non-finite values.
Results may differ from a plain program's by a relative error of at most 0.0059.
Values may be sent and summed in bfloat16 or wider, within the bound.
A program may use at most 192 MiB of HBM per device.

v0:
```python
import math

import jax
import jax.numpy as jnp
from jax import lax
from jax.sharding import PartitionSpec as P


def gelu_parts(hidden):
    coeff = math.sqrt(2.0 / math.pi)
    cubic = hidden * hidden * hidden
    tangent = jnp.tanh(coeff * (hidden + 0.044715 * cubic))
    value = 0.5 * hidden * (1.0 + tangent)
    slope = 0.5 * (1.0 + tangent) + 0.5 * hidden * (1.0 - tangent * tangent) * coeff * (
        1.0 + 3.0 * 0.044715 * hidden * hidden
    )
    return (value, slope)


def contract_last(left, right):
    return lax.dot_general(
        left, right, (((1,), (1,)), ((), ())), preferred_element_type=jnp.float32
    )


def contract_first(left, right):
    return lax.dot_general(
        left, right, (((0,), (0,)), ((), ())), preferred_element_type=jnp.float32
    )


def per_device(layer_input, w_in, w_out, output_grad):
    x_all, dy_all = (
        lax.all_gather(layer_input, "row", axis=0, tiled=True),
        lax.all_gather(output_grad, "row", axis=0, tiled=True),
    )
    rows = x_all
    hidden = lax.psum_scatter(
        jnp.dot(rows, w_in, preferred_element_type=jnp.float32),
        "col",
        scatter_dimension=0,
        tiled=True,
    )
    value, slope = gelu_parts(hidden)
    g_all = lax.all_gather(value.astype(jnp.bfloat16), "col", axis=0, tiled=True)
    rows = g_all
    mixed = lax.psum_scatter(
        jnp.dot(rows, w_out, preferred_element_type=jnp.float32),
        "row",
        scatter_dimension=0,
        tiled=True,
    )
    block_output = (layer_input.astype(jnp.float32) + mixed).astype(jnp.bfloat16)
    rows = dy_all
    grad_act = lax.psum_scatter(contract_last(rows, w_out), "col", scatter_dimension=0, tiled=True)
    grad_hid = (grad_act * slope).astype(jnp.bfloat16)
    dh_all = lax.all_gather(grad_hid, "col", axis=0, tiled=True)
    rows = dh_all
    back = lax.psum_scatter(contract_last(rows, w_in), "row", scatter_dimension=0, tiled=True)
    input_grad = (output_grad.astype(jnp.float32) + back).astype(jnp.bfloat16)
    part_in = contract_first(x_all, dh_all)
    part_out = contract_first(g_all, dy_all)
    total_in, total_out = (
        lax.psum(part_in.astype(jnp.bfloat16), "depth").astype(jnp.float32),
        lax.psum(part_out.astype(jnp.bfloat16), "depth").astype(jnp.float32),
    )
    return (block_output, input_grad, total_in.astype(jnp.bfloat16), total_out.astype(jnp.bfloat16))


def solution(mesh):
    in_specs = (
        P(("depth", "row"), "col"),
        P("col", "row"),
        P("row", "col"),
        P(("depth", "row"), "col"),
    )
    out_specs = (
        P(("depth", "row"), "col"),
        P(("depth", "row"), "col"),
        P("col", "row"),
        P("row", "col"),
    )
    return jax.shard_map(
        per_device, mesh=mesh, in_specs=in_specs, out_specs=out_specs, check_vma=False
    )
```

profile of v0, /device:TPU:0, one launch (start us, length us, event | category | flops | bytes accessed | tf_op | source)
XLA Modules:
  0.0 485.2 jit_solution(7489164302326343158)
XLA Ops:
  7.2 0.0 all-gather.9.cloned.1.call-start
  7.2 0.7 all-gather.9.cloned.1.call-update
  7.9 0.0 all-gather.5.cloned.1.call-start
  7.9 0.7 all-gather.5.cloned.1.call-update
  8.6 0.0 reduce-scatter.9.cloned.1.call-start
  8.7 49.2 %all-gather.9.cloned.1.call-done = bf16[512,2048]{1,0:T(8,128)(2,1)} async-done(((bf16[32,2048]{1,0:T(8,128)(2,1)}), bf16[512,2048]{1,0:T(8,128)(2,1)}) %all-gather.9.cloned.1.call-update) | async-done | bytes 2097168 | tf_op jit(solution)/shard_map/all_gather | solution.py:35
  57.9 8.5 %fusion.12 = f32[512,1536]{1,0:T(8,128)} fusion(bf16[512,2048]{1,0:T(8,128)(2,1)} %all-gather.9.cloned.1.call-done, bf16[1536,2048]{1,0:T(8,128)(2,1)} %param.6), kind=kOutput, calls=%fused_computation.19 | convolution fusion | flops 3221225472 | bytes 11534336 | tf_op jit(solution)/shard_map/dot_general | solution.py:21
  66.5 0.0 reduce-scatter.5.cloned.1.call-start
  66.5 38.1 %all-gather.5.cloned.1.call-done = bf16[512,2048]{1,0:T(8,128)(2,1)} async-done(((bf16[32,2048]{1,0:T(8,128)(2,1)}), bf16[512,2048]{1,0:T(8,128)(2,1)}) %all-gather.5.cloned.1.call-update) | async-done | bytes 2097168 | tf_op jit(solution)/shard_map/all_gather | solution.py:34
  104.6 8.5 %fusion.10 = f32[512,1536]{1,0:T(8,128)} fusion(bf16[512,2048]{1,0:T(8,128)(2,1)} %all-gather.5.cloned.1.call-done, bf16[2048,1536]{1,0:T(8,128)(2,1)} %param.5), kind=kOutput, calls=%fused_computation.17 | convolution fusion | flops 3221225472 | bytes 11534336 | tf_op jit(solution)/shard_map/dot_general | solution.py:39
  113.1 0.0 all-gather.7.cloned.1.call-start
  113.2 32.0 %reduce-scatter.9.cloned.1.call-done = f32[128,1536]{1,0:T(8,128)} async-done(((f32[512,1536]{1,0:T(8,128)}), f32[128,1536]{1,0:T(8,128)}) %reduce-scatter.9.cloned.1.call-update) | async-done | bytes 786448 | tf_op jit(solution)/shard_map/reduce_scatter | solution.py:55
  145.1 40.8 %reduce-scatter.5.cloned.1.call-done = f32[128,1536]{1,0:T(8,128)} async-done(((f32[512,1536]{1,0:T(8,128)}), f32[128,1536]{1,0:T(8,128)}) %reduce-scatter.5.cloned.1.call-update) | async-done | bytes 786448 | tf_op jit(solution)/shard_map/reduce_scatter | solution.py:38
  186.0 2.8 fusion.9
  188.8 0.0 all-gather.11.cloned.1.call-start
  188.8 0.5 all-gather.11.cloned.1.call-update
  189.4 0.0 reduce-scatter.7.cloned.1.call-start
  189.4 25.8 %all-gather.7.cloned.1.call-done = bf16[512,1536]{1,0:T(8,128)(2,1)} async-done(((bf16[128,1536]{1,0:T(8,128)(2,1)}), bf16[512,1536]{1,0:T(8,128)(2,1)}) %all-gather.7.cloned.1.call-update) | async-done | bytes 1572880 | tf_op jit(solution)/shard_map/all_gather | solution.py:45
  215.2 8.6 %fusion.11 = f32[512,2048]{1,0:T(8,128)} fusion(bf16[512,1536]{1,0:T(8,128)(2,1)} %all-gather.7.cloned.1.call-done, bf16[1536,2048]{1,0:T(8,128)(2,1)} %param.6), kind=kOutput, calls=%fused_computation.18 | convolution fusion | flops 3221225472 | bytes 12058624 | tf_op jit(solution)/shard_map/dot_general | solution.py:48
  223.8 0.0 reduce-scatter.11.cloned.1.call-start
  223.9 20.0 %all-gather.11.cloned.1.call-done = bf16[512,1536]{1,0:T(8,128)(2,1)} async-done(((bf16[128,1536]{1,0:T(8,128)(2,1)}), bf16[512,1536]{1,0:T(8,128)(2,1)}) %all-gather.11.cloned.1.call-update) | async-done | bytes 1572880 | tf_op jit(solution)/shard_map/all_gather | solution.py:57
  243.9 8.7 %fusion.13 = f32[512,2048]{1,0:T(8,128)} fusion(bf16[512,1536]{1,0:T(8,128)(2,1)} %all-gather.11.cloned.1.call-done, bf16[2048,1536]{1,0:T(8,128)(2,1)} %param.5), kind=kOutput, calls=%fused_computation.20 | convolution fusion | flops 3221225472 | bytes 12058624 | tf_op jit(solution)/shard_map/dot_general | solution.py:21
  252.6 0.2 all-reduce.3.cloned.1.call-start
  252.8 8.4 %fusion = bf16[2048,1536]{0,1:T(8,128)(2,1)} fusion(bf16[512,1536]{1,0:T(8,128)(2,1)} %all-gather.11.cloned.1.call-done, bf16[512,2048]{1,0:T(8,128)(2,1)} %all-gather.5.cloned.1.call-done), kind=kOutput, calls=%fused_computation.2 | convolution fusion | flops 3224371200 | bytes 9961472 | tf_op jit(solution)/shard_map/dot_general | solution.py:27
  261.2 5.3 %convolution_convert_fusion = bf16[1536,2048]{1,0:T(8,128)(2,1)} fusion(bf16[512,1536]{1,0:T(8,128)(2,1)S(1)} %copy-done.3, bf16[512,2048]{1,0:T(8,128)(2,1)S(1)} %copy-done.2), kind=kOutput, calls=%fused_computation | convolution fusion | flops 3224371200 | bytes 9961472 | tf_op jit(solution)/shard_map/dot_general | solution.py:27
  266.6 58.6 %reduce-scatter.7.cloned.1.call-done = f32[32,2048]{1,0:T(8,128)} async-done(((f32[512,2048]{1,0:T(8,128)}), f32[32,2048]{1,0:T(8,128)}) %reduce-scatter.7.cloned.1.call-update) | async-done | bytes 262160 | tf_op jit(solution)/shard_map/reduce_scatter | solution.py:47
  325.2 1.6 add_convert_fusion.1
  326.8 79.2 %reduce-scatter.11.cloned.1.call-done = f32[32,2048]{1,0:T(8,128)} async-done(((f32[512,2048]{1,0:T(8,128)}), f32[32,2048]{1,0:T(8,128)}) %reduce-scatter.11.cloned.1.call-update) | async-done | bytes 262160 | tf_op jit(solution)/shard_map/reduce_scatter | solution.py:59
  406.0 1.6 add_convert_fusion
  407.6 55.9 %all-reduce.3.cloned.1.call-done = (bf16[2048,1536]{0,1:T(8,128)(2,1)}, bf16[1536,2048]{1,0:T(8,128)(2,1)}) async-done(((bf16[2048,1536]{0,1:T(8,128)(2,1)}, bf16[1536,2048]{1,0:T(8,128)(2,1)}), (bf16[2048,1536]{0,1:T(8,128)(2,1)}, bf16[1536,2048]{1,0:T(8,128)(2,1)})) %all-reduce.3.cloned.1.call-update) | async-done | bytes 12582928 | tf_op jit(solution)/shard_map/psum | solution.py:64
  463.5 8.6 %copy.8 = bf16[2048,1536]{1,0:T(8,128)(2,1)} copy(bf16[2048,1536]{0,1:T(8,128)(2,1)} %get-tuple-element.8) | data formatting | bytes 12582912
  472.1 6.6 %copy.11 = bf16[1536,2048]{1,0:T(8,128)(2,1)} copy(bf16[1536,2048]{1,0:T(8,128)(2,1)} %get-tuple-element.15) | data formatting | bytes 12582912
  (14 shorter events, 0.1 us)
Async XLA Ops:
  7.2 50.7 %all-gather.9.cloned.1.call-start = ((), (), s32[]{:S(2)}) async-start(), calls=%async_computation.8 | async-start | bytes 2228224 | tf_op jit(solution)/shard_map/all_gather | solution.py:35
  7.9 96.7 %all-gather.5.cloned.1.call-start = ((), (), s32[]{:S(2)}) async-start(), calls=%async_computation.4 | async-start | bytes 2228224 | tf_op jit(solution)/shard_map/all_gather | solution.py:34
  8.6 136.5 %reduce-scatter.9.cloned.1.call-start = ((), (), s32[]{:S(2)}) async-start(), calls=%async_computation.9 | async-start | bytes 3932160 | tf_op jit(solution)/shard_map/reduce_scatter | solution.py:55
  66.5 119.5 %reduce-scatter.5.cloned.1.call-start = ((), (), s32[]{:S(2)}) async-start(), calls=%async_computation.5 | async-start | bytes 3932160 | tf_op jit(solution)/shard_map/reduce_scatter | solution.py:38
  113.1 102.1 %all-gather.7.cloned.1.call-start = ((), (), s32[]{:S(2)}) async-start(), calls=%async_computation.6 | async-start | bytes 1966080 | tf_op jit(solution)/shard_map/all_gather | solution.py:45
  188.8 55.1 %all-gather.11.cloned.1.call-start = ((), (), s32[]{:S(2)}) async-start(), calls=%async_computation.10 | async-start | bytes 1966080 | tf_op jit(solution)/shard_map/all_gather | solution.py:57
  189.4 135.8 %reduce-scatter.7.cloned.1.call-start = ((), (), s32[]{:S(2)}) async-start(), calls=%async_computation.7 | async-start | bytes 4456448 | tf_op jit(solution)/shard_map/reduce_scatter | solution.py:47
  223.8 182.1 %reduce-scatter.11.cloned.1.call-start = ((), (), s32[]{:S(2)}) async-start(), calls=%async_computation.11 | async-start | bytes 4456448 | tf_op jit(solution)/shard_map/reduce_scatter | solution.py:59
  252.6 8.6 %copy-start.2 = (bf16[512,2048]{1,0:T(8,128)(2,1)S(1)}, bf16[512,2048]{1,0:T(8,128)(2,1)}, u32[]{:S(2)}) copy-start(bf16[512,2048]{1,0:T(8,128)(2,1)} %all-gather.9.cloned.1.call-done) | copy-start | bytes 6291460
  252.6 210.9 %all-reduce.3.cloned.1.call-start = ((), (), s32[]{:S(2)}) async-start(), calls=%async_computation.12 | async-start | bytes 25165824 | tf_op jit(solution)/shard_map/psum | solution.py:64
  252.8 8.4 %copy-start.3 = (bf16[512,1536]{1,0:T(8,128)(2,1)S(1)}, bf16[512,1536]{1,0:T(8,128)(2,1)}, u32[]{:S(2)}) copy-start(bf16[512,1536]{1,0:T(8,128)(2,1)} %all-gather.7.cloned.1.call-done) | copy-start | bytes 4718596
  266.6 58.6 %copy-start = (bf16[32,2048]{1,0:T(8,128)(2,1)S(1)}, bf16[32,2048]{1,0:T(8,128)(2,1)}, u32[]{:S(2)}) copy-start(bf16[32,2048]{1,0:T(8,128)(2,1)} %param.4) | copy-start | bytes 393220
  266.6 139.4 %copy-start.1 = (bf16[32,2048]{1,0:T(8,128)(2,1)S(1)}, bf16[32,2048]{1,0:T(8,128)(2,1)}, u32[]{:S(2)}) copy-start(bf16[32,2048]{1,0:T(8,128)(2,1)} %param.7) | copy-start | bytes 393220
Sparse Core Ops, SparseCore 0:
  10.1 47.7 all-gather.8
  60.0 44.5 all-gather.4
  107.6 37.5 reduce-scatter.8
  148.0 37.9 reduce-scatter.4
  188.9 26.2 all-gather.6
  217.3 26.5 all-gather.10
  247.2 77.8 reduce-scatter.6
  328.9 77.0 reduce-scatter.10
  409.2 54.2 all-reduce.2
where the time goes:
time: 487 us; the launch traced here: 485 us
  waiting for transfers between devices  402 us (83%)
  matrix products  48 us (10%)
  local copies, waits for them, and re-layouts  15.2 us (3%)
  between operations  13.9 us (3%)
  other arithmetic  6.04 us (1%)
    reduce_scatter x1, waiting for transfers between devices, per_device(): lax.psum_scatter(contract_last(rows, w_in), 'row', scatter_dimension=0, t...  79.2 us
    reduce_scatter x1, waiting for transfers between devices, per_device(): lax.psum_scatter(jnp.dot(rows, w_out, preferred_element_type=jnp.float32)...  58.6 us
    psum x1, waiting for transfers between devices, per_device(): lax.psum(part_in.astype(jnp.bfloat16), 'depth').astype(jnp.float32)  55.9 us
    all_gather x1, waiting for transfers between devices, per_device(): lax.all_gather(output_grad, 'row', axis=0, tiled=True)  49.2 us
    reduce_scatter x1, waiting for transfers between devices, per_device(): lax.psum_scatter(jnp.dot(rows, w_in, preferred_element_type=jnp.float32),...  40.8 us
    all_gather x1, waiting for transfers between devices, per_device(): lax.all_gather(layer_input, 'row', axis=0, tiled=True)  38.1 us
    reduce_scatter x1, waiting for transfers between devices, per_device(): lax.psum_scatter(contract_last(rows, w_out), 'col', scatter_dimension=0,...  32 us
    all_gather x1, waiting for transfers between devices, per_device(): lax.all_gather(value.astype(jnp.bfloat16), 'col', axis=0, tiled=True)  25.8 us
  transfers between devices with their start and end apart: 9, of which 9 were waited for; matrix products, arithmetic and copies ran while one was open for 11% of the time, Pallas kernels for 0%

commit v1 on v0

v1 whole, which is shorter than its diff:
```python
import math

import jax
import jax.numpy as jnp
from jax import lax
from jax.experimental import pallas as pl
from jax.experimental.pallas import tpu as pltpu
from jax.sharding import PartitionSpec as P

MESH = pl.DeviceIdType.MESH
SIDE = 4
OWN, PREV, NEXT, FAR = range(4)
CHUNKS = (
    ((OWN, 0, 4),),
    ((PREV, 0, 2), (NEXT, 0, 2)),
    ((PREV, 2, 4), (NEXT, 2, 4)),
    ((FAR, 0, 4),),
)
LO, HI = pl.ds(0, 2), pl.ds(2, 2)
TOP, END = pl.ds(0, 16), pl.ds(16, 16)
N_SEMS = 420


def gelu_parts(hidden):
    coeff = math.sqrt(2.0 / math.pi)
    square = hidden * hidden
    tangent = jnp.tanh(coeff * (hidden + 0.044715 * (square * hidden)))
    value = 0.5 * hidden * (1.0 + tangent)
    slope = 0.5 * (1.0 + tangent) + 0.5 * hidden * (1.0 - tangent * tangent) * coeff * (
        1.0 + 3.0 * 0.044715 * square
    )
    return (value, slope)


def f32(value):
    return value.astype(jnp.float32)


def b16(value):
    return value.astype(jnp.bfloat16)


class Ring:
    def __init__(self, after, before):
        self.after = after
        self.before = before


def block_kernel(
    x_ref, dy_ref, w_in_hbm, w_out_hbm,
    out_ref, grad_ref, x_hbm, dy_hbm, g_hbm, dh_hbm,
    w_in, w_out, x_all, dy_all, g_all, dh_all, slope,
    ysum, yfwd, yback, zsum, zfwd, zback, zown, xsum, xfwd, xback,
    sems,
):
    layer = lax.axis_index("depth")
    row = lax.axis_index("row")
    col = lax.axis_index("col")
    across, along = row // SIDE, row % SIDE

    def device(d, i, k, c):
        return (d, ((i + SIDE) % SIDE) * SIDE + (k + SIDE) % SIDE, (c + SIDE) % SIDE)

    ring_x = Ring(device(layer, across + 1, along, col), device(layer, across - 1, along, col))
    ring_z = Ring(device(layer, across, along + 1, col), device(layer, across, along - 1, col))
    ring_y = Ring(device(layer, across, along, col + 1), device(layer, across, along, col - 1))
    twin = (1 - layer, row, col)

    count = [0]
    sent = []

    def sem():
        count[0] += 1
        return sems.at[count[0] - 1]

    def send(src, dst, to):
        copy = pltpu.make_async_remote_copy(
            src_ref=src, dst_ref=dst, send_sem=sem(), recv_sem=sem(),
            device_id=to, device_id_type=MESH,
        )
        copy.start()
        sent.append(copy.wait_send)
        return copy

    def local(src, dst):
        copy = pltpu.make_async_copy(src, dst, sem())
        copy.start()
        return copy

    load_in = local(w_in_hbm, w_in)
    load_out = local(w_out_hbm, w_out)

    barrier = pltpu.get_barrier_semaphore()
    greeted = (ring_x.after, ring_x.before, ring_z.after, ring_z.before)
    greeted += (ring_y.after, ring_y.before, twin)
    for other in greeted:
        pl.semaphore_signal(barrier, inc=1, device_id=other, device_id_type=MESH)
    x_all[OWN, OWN] = x_ref[...]
    dy_all[OWN, OWN] = dy_ref[...]
    pl.semaphore_wait(barrier, len(greeted))

    def first_sends(every, ring):
        own = every.at[OWN, OWN]
        return (
            send(own, every.at[OWN, PREV], ring.after),
            send(own, every.at[OWN, NEXT], ring.before),
        )

    def plane_send(every, ring, block):
        own = every.at[OWN, block]
        return (
            send(own, every.at[PREV, block], ring.after),
            send(own, every.at[NEXT, block], ring.before),
        )

    stage1_x = first_sends(x_all, ring_x)
    stage1_dy = first_sends(dy_all, ring_z)
    planes_x = [plane_send(x_all, ring_z, OWN)]
    planes_dy = [plane_send(dy_all, ring_x, OWN)]
    far_x, far_dy = [], []
    for every, stage1, planes, far, first, second in (
        (x_all, stage1_x, planes_x, far_x, ring_x, ring_z),
        (dy_all, stage1_dy, planes_dy, far_dy, ring_z, ring_x),
    ):
        stage1[0].wait_recv()
        far.append(send(every.at[OWN, PREV, TOP], every.at[OWN, FAR, TOP], first.after))
        planes.append(plane_send(every, second, PREV))
        stage1[1].wait_recv()
        far.append(send(every.at[OWN, NEXT, END], every.at[OWN, FAR, END], first.before))
        planes.append(plane_send(every, second, NEXT))
    for every, planes, far, second in (
        (x_all, planes_x, far_x, ring_z),
        (dy_all, planes_dy, far_dy, ring_x),
    ):
        far[0].wait_recv()
        far[1].wait_recv()
        planes.append(plane_send(every, second, FAR))

    width = slope.shape[-1]

    def rows_of(every, chunk):
        parts = [every[plane, pl.ds(lo, hi - lo)] for plane, lo, hi in CHUNKS[chunk]]
        part = parts[0] if len(parts) == 1 else jnp.concatenate(parts, axis=0)
        return part.reshape(part.shape[0] * part.shape[1], part.shape[2])

    def y_product(kind, chunk):
        mine = ysum.at[kind, chunk]
        every = (x_all, dy_all)[kind]

        @pl.loop(0, 2)
        def _(tile):
            span = pl.ds(pl.multiple_of(tile * 2 * width, 2 * width), 2 * width)
            lhs = rows_of(every, chunk)
            if kind == 0:
                part = jnp.dot(lhs, w_in[:, span], preferred_element_type=jnp.float32)
            else:
                part = lax.dot_general(
                    lhs, w_out[span, :], (((1,), (1,)), ((), ())),
                    preferred_element_type=jnp.float32,
                )
            part = b16(part)
            for half in range(2):
                shard = (2 * tile + half + SIDE - col) % SIDE
                cut = part[:, half * width : (half + 1) * width]
                mine[shard] = cut.reshape(4, cut.shape[0] // 4, width)

        fwd, back = yfwd.at[kind, chunk], yback.at[kind, chunk]
        return [
            send(mine.at[2, HI], fwd.at[0], ring_y.after),
            send(mine.at[2, LO], fwd.at[1], ring_y.before),
            send(mine.at[1, LO], back.at[0, LO], ring_y.after),
            send(mine.at[3, HI], back.at[1, HI], ring_y.before),
        ]

    def y_relay(kind, chunk, copies):
        mine, fwd, back = ysum.at[kind, chunk], yfwd.at[kind, chunk], yback.at[kind, chunk]
        copies[0].wait_recv()
        mine[1, HI] = b16(f32(mine[1, HI]) + f32(fwd[0]))
        copies.append(send(mine.at[1, HI], back.at[0, HI], ring_y.after))
        copies[1].wait_recv()
        mine[3, LO] = b16(f32(mine[3, LO]) + f32(fwd[1]))
        copies.append(send(mine.at[3, LO], back.at[1, LO], ring_y.before))

    def y_total(kind, chunk, copies):
        for copy in copies[2:]:
            copy.wait_recv()
        mine, back = ysum.at[kind, chunk], yback.at[kind, chunk]
        return f32(mine[0]) + f32(back[0]) + f32(back[1])

    own_columns = pl.ds(pl.multiple_of(col * width, width), width)

    def finish_hidden(chunk, copies):
        value, steep = gelu_parts(y_total(0, chunk, copies))
        value = b16(value)
        at = 0
        for plane, lo, hi in CHUNKS[chunk]:
            g_all[plane, pl.ds(lo, hi - lo), :, own_columns] = value[at : at + hi - lo]
            slope[plane, pl.ds(lo, hi - lo)] = steep[at : at + hi - lo]
            at += hi - lo

    def finish_grad(chunk, copies):
        total = y_total(1, chunk, copies)
        at = 0
        for plane, lo, hi in CHUNKS[chunk]:
            for block in range(lo, hi):
                dh_all[plane, block, :, own_columns] = b16(total[at] * slope[block, plane])
                at += 1

    def gather_wait(planes, block):
        for copy in planes[block]:
            copy.wait_recv()

    c = {}
    load_in.wait()
    c["h0"] = y_product(0, 0)
    load_out.wait()
    c["a0"] = y_product(1, 0)
    fars = {}
    for every, planes, second, name in (
        (x_all, planes_x, ring_z, "x"), (dy_all, planes_dy, ring_x, "dy"),
    ):
        gather_wait(planes, OWN)
        gather_wait(planes, PREV)
        fars[name] = [send(every.at[PREV, LO], every.at[FAR, LO], second.after)]
    c["h1"] = y_product(0, 1)
    y_relay(0, 0, c["h0"])
    c["a1"] = y_product(1, 1)
    y_relay(1, 0, c["a0"])
    for every, planes, second, name in (
        (x_all, planes_x, ring_z, "x"), (dy_all, planes_dy, ring_x, "dy"),
    ):
        gather_wait(planes, NEXT)
        gather_wait(planes, FAR)
        fars[name].append(send(every.at[NEXT, HI], every.at[FAR, HI], second.before))
    c["h2"] = y_product(0, 2)
    y_relay(0, 1, c["h1"])
    c["a2"] = y_product(1, 2)
    y_relay(1, 1, c["a1"])
    finish_hidden(0, c["h0"])
    for copy in fars["x"]:
        copy.wait_recv()
    c["h3"] = y_product(0, 3)
    y_relay(0, 2, c["h2"])
    for copy in fars["dy"]:
        copy.wait_recv()
    c["a3"] = y_product(1, 3)

    keep = []
    shared = []
    for plane in range(4):
        keep.append(local(x_all.at[plane], x_hbm.at[layer, plane]))
        shared.append(send(x_all.at[plane], x_hbm.at[layer, plane], twin))
        keep.append(local(dy_all.at[plane], dy_hbm.at[layer, :, plane]))
        shared.append(send(dy_all.at[plane], dy_hbm.at[layer, :, plane], twin))

    y_relay(1, 2, c["a2"])
    finish_hidden(1, c["h1"])
    finish_hidden(2, c["h2"])

    def y_gather(every, plane):
        own = every.at[plane, :, :, own_columns]
        return [send(own, own, ring_y.after), send(own, own, ring_y.before)]

    def columns_of(step):
        at = (col + step + SIDE) % SIDE
        return pl.ds(pl.multiple_of(at * width, width), width)

    def y_pass(every, plane, copies):
        copies[0].wait_recv()
        part = every.at[plane, LO, :, columns_of(-1)]
        copies.append(send(part, part, ring_y.after))
        copies[1].wait_recv()
        part = every.at[plane, HI, :, columns_of(1)]
        copies.append(send(part, part, ring_y.before))

    def product(kind, plane):
        every = (g_all, dh_all)[kind]

        @pl.loop(0, 4)
        def _(tile):
            cols = w_out.shape[1] // 4
            span = pl.ds(pl.multiple_of(tile * cols, cols), cols)
            lhs = every[plane].reshape(-1, every.shape[-1])
            if kind == 0:
                part = jnp.dot(lhs, w_out[:, span], preferred_element_type=jnp.float32)
            else:
                part = lax.dot_general(
                    lhs, w_in[span, :], (((1,), (1,)), ((), ())),
                    preferred_element_type=jnp.float32,
                )
            part = part.reshape(4, part.shape[0] // 4, cols)
            if plane == OWN:
                zown[kind, :, :, span] = part
            else:
                zsum[kind, plane, :, :, span] = b16(part)

    def planes_start(kind, plane, ring):
        mine, fwd, back = zsum.at[kind], zfwd.at[kind], zback.at[kind]
        if plane == FAR:
            return [
                send(mine.at[FAR, HI], fwd.at[0], ring.after),
                send(mine.at[FAR, LO], fwd.at[1], ring.before),
            ]
        if plane == NEXT:
            return [send(mine.at[NEXT, LO], back.at[0, LO], ring.after)]
        return [send(mine.at[PREV, HI], back.at[1, HI], ring.before)]

    def planes_relay(kind, copies, ring):
        mine, fwd, back = zsum.at[kind], zfwd.at[kind], zback.at[kind]
        copies[FAR][0].wait_recv()
        mine[NEXT, HI] = b16(f32(mine[NEXT, HI]) + f32(fwd[0]))
        copies[NEXT].append(send(mine.at[NEXT, HI], back.at[0, HI], ring.after))
        copies[FAR][1].wait_recv()
        mine[PREV, LO] = b16(f32(mine[PREV, LO]) + f32(fwd[1]))
        copies[PREV].append(send(mine.at[PREV, LO], back.at[1, LO], ring.before))

    def blocks_start(kind, copies, ring):
        for copy in copies[NEXT] + copies[PREV]:
            copy.wait_recv()
        for block in (FAR, NEXT, PREV, OWN):
            total = zown[kind, block] + f32(zback[kind, 0, block]) + f32(zback[kind, 1, block])
            if block == OWN:
                zown[kind, OWN] = total
            else:
                xsum[kind, block] = b16(total)
        mine, fwd, back = xsum.at[kind], xfwd.at[kind], xback.at[kind]
        return [
            send(mine.at[FAR, END], fwd.at[0], ring.after),
            send(mine.at[FAR, TOP], fwd.at[1], ring.before),
            send(mine.at[NEXT, TOP], back.at[0, TOP], ring.after),
            send(mine.at[PREV, END], back.at[1, END], ring.before),
        ]

    def blocks_relay(kind, copies, ring):
        mine, fwd, back = xsum.at[kind], xfwd.at[kind], xback.at[kind]
        copies[0].wait_recv()
        mine[NEXT, END] = b16(f32(mine[NEXT, END]) + f32(fwd[0]))
        copies.append(send(mine.at[NEXT, END], back.at[0, END], ring.after))
        copies[1].wait_recv()
        mine[PREV, TOP] = b16(f32(mine[PREV, TOP]) + f32(fwd[1]))
        copies.append(send(mine.at[PREV, TOP], back.at[1, TOP], ring.before))

    def blocks_total(kind, copies):
        for copy in copies[2:]:
            copy.wait_recv()
        return zown[kind, OWN] + f32(xback[kind, 0]) + f32(xback[kind, 1])

    passes = {}
    moves = {0: {}, 1: {}}
    rings = (ring_z, ring_x)

    def start(name):
        kind, plane = name
        passes[name] = y_gather((g_all, dh_all)[kind], plane)

    def relay(name):
        kind, plane = name
        y_pass((g_all, dh_all)[kind], plane, passes[name])

    def finish(name):
        kind, plane = name
        for copy in passes[name][2:]:
            copy.wait_recv()
        every, kept = ((g_all, g_hbm), (dh_all, dh_hbm))[kind]
        to = kept.at[layer, plane] if kind == 0 else kept.at[layer, :, plane]
        keep.append(local(every.at[plane], to))
        shared.append(send(every.at[plane], to, twin))
        product(kind, plane)
        if plane != OWN:
            moves[kind][plane] = planes_start(kind, plane, rings[kind])

    start((0, PREV))
    y_relay(0, 3, c["h3"])
    start((0, NEXT))
    y_relay(1, 3, c["a3"])
    finish_hidden(3, c["h3"])
    relay((0, PREV))
    start((0, FAR))
    for chunk in range(4):
        finish_grad(chunk, c["a" + str(chunk)])
    relay((0, NEXT))
    start((1, FAR))
    finish((0, PREV))
    relay((0, FAR))
    start((1, NEXT))
    finish((0, NEXT))
    relay((1, FAR))
    start((1, PREV))
    finish((0, FAR))
    relay((1, NEXT))
    start((0, OWN))
    finish((1, FAR))
    planes_relay(0, moves[0], ring_z)
    relay((1, PREV))
    start((1, OWN))
    finish((1, NEXT))
    relay((0, OWN))
    finish((1, PREV))
    relay((1, OWN))
    planes_relay(1, moves[1], ring_x)
    finish((0, OWN))
    last_out = blocks_start(0, moves[0], ring_x)
    finish((1, OWN))
    last_grad = blocks_start(1, moves[1], ring_z)
    blocks_relay(0, last_out, ring_x)
    blocks_relay(1, last_grad, ring_z)
    out_ref[...] = f32(x_ref[...]) + blocks_total(0, last_out)
    grad_ref[...] = f32(dy_ref[...]) + blocks_total(1, last_grad)

    for copy in keep:
        copy.wait()
    for copy in shared:
        copy.wait_recv()
    for wait_send in sent:
        wait_send()


def run_block(x, dy, w_in, w_out):
    tokens, features = x.shape
    hidden = w_in.shape[1]
    width = hidden // SIDE
    every = (4, 4, tokens, features)
    bf, fl = jnp.bfloat16, jnp.float32
    vmem = pl.BlockSpec(memory_space=pltpu.VMEM)
    hbm = pl.BlockSpec(memory_space=pl.ANY)
    shape = jax.ShapeDtypeStruct
    return pl.pallas_call(
        block_kernel,
        out_shape=(
            shape((tokens, features), fl),
            shape((tokens, features), fl),
            shape((2,) + every, bf),
            shape((2,) + every, bf),
            shape((2, 4, 4, tokens, hidden), bf),
            shape((2, 4, 4, tokens, hidden), bf),
        ),
        in_specs=[vmem, vmem, hbm, hbm],
        out_specs=(vmem, vmem, hbm, hbm, hbm, hbm),
        scratch_shapes=[
            pltpu.VMEM(w_in.shape, bf),
            pltpu.VMEM(w_out.shape, bf),
            pltpu.VMEM(every, bf),
            pltpu.VMEM(every, bf),
            pltpu.VMEM((4, 4, tokens, hidden), bf),
            pltpu.VMEM((4, 4, tokens, hidden), bf),
            pltpu.VMEM((4, 4, tokens, width), fl),
            pltpu.VMEM((2, 4, 4, 4, tokens, width), bf),
            pltpu.VMEM((2, 4, 2, 2, tokens, width), bf),
            pltpu.VMEM((2, 4, 2, 4, tokens, width), bf),
            pltpu.VMEM((2,) + every, bf),
            pltpu.VMEM((2, 2, 2, tokens, features), bf),
            pltpu.VMEM((2, 2, 4, tokens, features), bf),
            pltpu.VMEM((2, 4, tokens, features), fl),
            pltpu.VMEM((2, 4, tokens, features), bf),
            pltpu.VMEM((2, 2, tokens // 2, features), bf),
            pltpu.VMEM((2, 2, tokens, features), bf),
            pltpu.SemaphoreType.DMA((N_SEMS,)),
        ],
        compiler_params=pltpu.CompilerParams(
            collective_id=1, has_side_effects=True, vmem_limit_bytes=60 * 2**20
        ),
    )(x, dy, w_in, w_out)


def contract_first(left, right):
    return lax.dot_general(
        left, right, (((0,), (0,)), ((), ())), preferred_element_type=jnp.float32
    )


def per_device(layer_input, w_in, w_out, output_grad):
    out, grad, x_all, dy_all, g_all, dh_all = run_block(layer_input, output_grad, w_in, w_out)
    features, hidden = w_in.shape
    w_in_grad = contract_first(x_all.reshape(-1, features), dh_all.reshape(-1, hidden))
    w_out_grad = contract_first(g_all.reshape(-1, hidden), dy_all.reshape(-1, features))
    return (b16(out), b16(grad), b16(w_in_grad), b16(w_out_grad))


def solution(mesh):
    in_specs = (
        P(("depth", "row"), "col"),
        P("col", "row"),
        P("row", "col"),
        P(("depth", "row"), "col"),
    )
    out_specs = (
        P(("depth", "row"), "col"),
        P(("depth", "row"), "col"),
        P("col", "row"),
        P("row", "col"),
    )
    return jax.shard_map(
        per_device, mesh=mesh, in_specs=in_specs, out_specs=out_specs, check_vma=False
    )
```

time: 487 us -> 126 us (0.26)
  waiting for transfers between devices: 402 us -> 0 us
  Pallas kernels: 0 us -> 102 us
  matrix products: 48 us -> 20.3 us
  local copies, waits for them, and re-layouts: 15.2 us -> 0.01 us
  between operations: 13.9 us -> 0.64 us
    reduce_scatter x4 -> x0, waiting for transfers between devices: 211 us -> none  [the longest x1 79.2 us: per_device(): lax.psum_scatter(contract_last(rows, w_in), 'row', scatter_dimension=0, t...]
    all_gather x4 -> x0, waiting for transfers between devices: 133 us -> none  [the longest x1 49.2 us: per_device(): lax.all_gather(output_grad, 'row', axis=0, tiled=True)]
    pallas_call x0 -> x1, Pallas kernels: none -> 102 us  [run_block(): pl.pallas_call(block_kernel, out_shape=(shape((tokens, features), fl), sh...]
    psum x1 -> x0, waiting for transfers between devices: 55.9 us -> none  [per_device(): lax.psum(part_in.astype(jnp.bfloat16), 'depth').astype(jnp.float32)]
    dot_general x4 -> x0, matrix products: 34.3 us -> none  [the longest x2 17.2 us: contract_last(): lax.dot_general(left, right, (((1,), (1,)), ((), ())), preferred_element_...]
    unnamed x10 -> x4, local copies, waits for them, and re-layouts: 15.2 us -> 0.01 us
    dot_general x2, matrix products: 13.7 us -> 20.3 us  [contract_first(): lax.dot_general(left, right, (((0,), (0,)), ((), ())), preferred_element_...]
  transfers between devices with their start and end apart: 9 -> 0, of which waited for: 9 -> 0; matrix products, arithmetic and copies ran while one was open for 11% -> 0% of each run, Pallas kernels for 0% -> 0%
where the time goes in v1:
time: 126 us
  Pallas kernels  102 us (81%)
  matrix products  20.3 us (16%)
  other arithmetic  3.24 us (3%)
    pallas_call x1, Pallas kernels, run_block(): pl.pallas_call(block_kernel, out_shape=(shape((tokens, features), fl), sh...  102 us
    dot_general x2, matrix products, contract_first(): lax.dot_general(left, right, (((0,), (0,)), ((), ())), preferred_element_...  20.3 us
    convert_element_type x2, other arithmetic, b16(): return value.astype(jnp.bfloat16)  3.24 us

profile of v1, /device:TPU:0, one launch (start us, length us, event | category | flops | bytes accessed | tf_op | source)
XLA Modules:
  0.0 126.0 jit_solution(8449056724083554704)
XLA Ops:
  0.6 101.8 %shard_map.75 = (f32[32,2048]{1,0:T(8,128)}, f32[32,2048]{1,0:T(8,128)}, bf16[2,4,4,32,2048]{4,3,2,1,0:T(8,128)(2,1)}, bf16[2,4,4,32,2048]{4,3,2,1,0:T(8,128)(2,...) custom-call(bf16[32,2048]{1,0:T(8,128)(2,1)} %x_ref.1, bf16[32,2048]{1,0:T(8,128)(2,1)} %dy_ref.1, ...), custom_call_target="tpu_custom_call" | custom-call | tf_op jit(solution)/shard_map/pallas_call | solution.py:427
  102.4 1.6 %convert_element_type.12 = bf16[32,2048]{1,0:T(8,128)(2,1)} convert(f32[32,2048]{1,0:T(8,128)} %get-tuple-element.10) | non-fusion elementwise | flops 65536 | bytes 393216 | tf_op jit(solution)/shard_map/convert_element_type | solution.py:40
  104.1 1.6 %convert_element_type.13 = bf16[32,2048]{1,0:T(8,128)(2,1)} convert(f32[32,2048]{1,0:T(8,128)} %get-tuple-element.11) | non-fusion elementwise | flops 65536 | bytes 393216 | tf_op jit(solution)/shard_map/convert_element_type | solution.py:40
  105.7 0.0 copy-start
  105.7 0.0 copy-start.1
  105.7 11.6 %bitcast_convert_fusion.1 = bf16[2048,1536]{1,0:T(8,128)(2,1)} fusion(bf16[2,4,4,32,2048]{4,3,2,1,0:T(8,128)(2,1)} %get-tuple-element.12, bf16[2,4,4,32,1536]{4,3,2,1,0:T(8,128)(2,1)} %get-tuple-element.13), kind=kOutput, calls=%fused_computation.1 | convolution fusion | flops 6445596672 | bytes 13631488 | tf_op jit(solution)/shard_map/dot_general | solution.py:466
  117.2 0.0 copy-done
  117.2 0.0 copy-done.1
  117.2 8.8 %bitcast_convert_fusion = bf16[1536,2048]{1,0:T(8,128)(2,1)} fusion(bf16[2,4,4,32,1536]{4,3,2,1,0:T(8,128)(2,1)S(1)} %copy-done.1, bf16[2,4,4,32,2048]{4,3,2,1,0:T(8,128)(2,1)S(1)} %copy-done), kind=kOutput, calls=%fused_computation | convolution fusion | flops 6445596672 | bytes 13631488 | tf_op jit(solution)/shard_map/dot_general | solution.py:466
Async XLA Ops:
  105.7 11.6 %copy-start = (bf16[2,4,4,32,2048]{4,3,2,1,0:T(8,128)(2,1)S(1)}, bf16[2,4,4,32,2048]{4,3,2,1,0:T(8,128)(2,1)}, u32[]{:S(2)}) copy-start(bf16[2,4,4,32,2048]{4,3,2,1,0:T(8,128)(2,1)} %get-tuple-element.15) | copy-start | bytes 12582916
  105.7 11.6 %copy-start.1 = (bf16[2,4,4,32,1536]{4,3,2,1,0:T(8,128)(2,1)S(1)}, bf16[2,4,4,32,1536]{4,3,2,1,0:T(8,128)(2,1)}, u32[]{:S(2)}) copy-start(bf16[2,4,4,32,1536]{4,3,2,1,0:T(8,128)(2,1)} %get-tuple-element.14) | copy-start | bytes 9437188

commit v2 on v0

v2 whole, which is shorter than its diff:
```python
import math

import jax
import jax.numpy as jnp
from jax import lax
from jax.experimental import pallas as pl
from jax.experimental.pallas import tpu as pltpu
from jax.sharding import PartitionSpec as P

MESH = pl.DeviceIdType.MESH
SIDE = 4
OWN, PREV, NEXT, FAR = range(4)
UNITS = (
    (
        ((OWN, 0, 3), (PREV, 0, 1), (NEXT, 0, 1)),
        ((OWN, 3, 4), (PREV, 1, 4), (NEXT, 1, 4), (FAR, 0, 4)),
    ),
    (((OWN, 0, 4), (PREV, 0, 4), (NEXT, 0, 4), (FAR, 0, 4)),),
)
SIZES = tuple(tuple(sum(hi - lo for _, lo, hi in unit) for unit in units) for units in UNITS)
STARTS = tuple(tuple(sum(sizes[:unit]) for unit in range(len(sizes))) for sizes in SIZES)
HALF = 16
LO, HI = pl.ds(0, 2), pl.ds(2, 2)
GROUPS = {"all": (OWN, 4), "others": (PREV, 3), "own": (OWN, 1)}
N_SEMS = 560


def gelu_parts(hidden):
    coeff = math.sqrt(2.0 / math.pi)
    square = hidden * hidden
    tangent = jnp.tanh(coeff * (hidden + 0.044715 * (square * hidden)))
    value = 0.5 * hidden * (1.0 + tangent)
    slope = 0.5 * (1.0 + tangent) + 0.5 * hidden * (1.0 - tangent * tangent) * coeff * (
        1.0 + 3.0 * 0.044715 * square
    )
    return (value, slope)


def f32(value):
    return value.astype(jnp.float32)


def b16(value):
    return value.astype(jnp.bfloat16)


class Ring:
    def __init__(self, after, before):
        self.after = after
        self.before = before


def block_kernel(
    x_ref, dy_ref, w_in_hbm, w_out_hbm,
    out_ref, grad_ref, x_hbm, dh_hbm, w_out_grad_hbm,
    w_in, w_out, x_all, dy_all, g_all, dh_all, slope, g_two, dy_two, w_out_grad,
    ysum, yfwd, yback, zsum, zfwd, zback, zown, xsum, xfwd, xback,
    sems,
):
    layer = lax.axis_index("depth")
    row = lax.axis_index("row")
    col = lax.axis_index("col")
    across, along = row // SIDE, row % SIDE

    def device(d, i, k, c):
        return (d, ((i + SIDE) % SIDE) * SIDE + (k + SIDE) % SIDE, (c + SIDE) % SIDE)

    ring_x = Ring(device(layer, across + 1, along, col), device(layer, across - 1, along, col))
    ring_z = Ring(device(layer, across, along + 1, col), device(layer, across, along - 1, col))
    ring_y = Ring(device(layer, across, along, col + 1), device(layer, across, along, col - 1))
    twin = (1 - layer, row, col)

    count = [0]
    sent = []

    def sem():
        count[0] += 1
        return sems.at[count[0] - 1]

    def send(src, dst, to):
        copy = pltpu.make_async_remote_copy(
            src_ref=src, dst_ref=dst, send_sem=sem(), recv_sem=sem(),
            device_id=to, device_id_type=MESH,
        )
        copy.start()
        sent.append(copy.wait_send)
        return copy

    def local(src, dst):
        copy = pltpu.make_async_copy(src, dst, sem())
        copy.start()
        return copy

    load_in = local(w_in_hbm, w_in)
    load_out = local(w_out_hbm, w_out)

    barrier = pltpu.get_barrier_semaphore()
    greeted = (ring_x.after, ring_x.before, ring_z.after, ring_z.before)
    greeted += (ring_y.after, ring_y.before, twin)
    for other in greeted:
        pl.semaphore_signal(barrier, inc=1, device_id=other, device_id_type=MESH)
    for half in range(2):
        rows = pl.ds(half * HALF, HALF)
        x_all[half, OWN, OWN] = x_ref[rows]
        dy_all[half, OWN, OWN] = dy_ref[rows]
    pl.semaphore_wait(barrier, len(greeted))

    kinds = ((x_all, ring_x, ring_z), (dy_all, ring_z, ring_x))
    features = x_all.shape[-1]
    left, right = pl.ds(0, features // 2), pl.ds(features // 2, features // 2)
    lines = {}
    planes = {}

    def share_block(kind, half, block):
        every, _, ring = kinds[kind]
        own = every.at[half, OWN, block]
        planes[kind, half, PREV, block] = send(own, every.at[half, PREV, block], ring.after)
        planes[kind, half, NEXT, block] = send(own, every.at[half, NEXT, block], ring.before)

    def open_line(kind, half):
        every, ring, _ = kinds[kind]
        own = every.at[half, OWN, OWN]
        lines[kind, half, PREV] = send(own, every.at[half, OWN, PREV], ring.after)
        lines[kind, half, NEXT] = send(own, every.at[half, OWN, NEXT], ring.before)

    def take_line(kind, half):
        every, ring, _ = kinds[kind]
        line = every.at[half, OWN]
        lines[kind, half, PREV].wait_recv()
        first = send(line.at[PREV, :, left], line.at[FAR, :, left], ring.after)
        lines[kind, half, NEXT].wait_recv()
        second = send(line.at[NEXT, :, right], line.at[FAR, :, right], ring.before)
        lines[kind, half, FAR] = (first, second)
        share_block(kind, half, PREV)
        share_block(kind, half, NEXT)

    def take_line_far(kind, half):
        for copy in lines[kind, half, FAR]:
            copy.wait_recv()
        share_block(kind, half, FAR)

    def take_block(kind, half, block):
        every, _, ring = kinds[kind]
        mine = every.at[half]
        planes[kind, half, PREV, block].wait_recv()
        if block in (OWN, PREV):
            copy = send(mine.at[PREV, block], mine.at[FAR, block], ring.after)
        planes[kind, half, NEXT, block].wait_recv()
        if block in (NEXT, FAR):
            copy = send(mine.at[NEXT, block], mine.at[FAR, block], ring.before)
        planes[kind, half, FAR, block] = copy

    def take_far(kind, half):
        for block in range(SIDE):
            planes[kind, half, FAR, block].wait_recv()

    for kind in range(2):
        open_line(kind, 0)
    for kind in range(2):
        share_block(kind, 0, OWN)

    width = slope.shape[-1]

    def rows_of(every, half, unit):
        parts = [every[half, plane, pl.ds(lo, hi - lo)] for plane, lo, hi in UNITS[half][unit]]
        part = parts[0] if len(parts) == 1 else jnp.concatenate(parts, axis=0)
        return part.reshape(part.shape[0] * part.shape[1], part.shape[2])

    def y_buffers(kind, half, unit):
        span = pl.ds(STARTS[half][unit], SIZES[half][unit])
        size = SIZES[half][unit]
        low, high = pl.ds(0, (size + 1) // 2), pl.ds((size + 1) // 2, size // 2)
        mine, fwd, back = ysum.at[kind, half, :, span], yfwd.at[kind, half], yback.at[kind, half]
        return mine, fwd.at[:, span], back.at[:, span], low, high

    sums = {}

    def y_product(kind, half, unit):
        mine, fwd, back, low, high = y_buffers(kind, half, unit)
        every = (x_all, dy_all)[kind]

        @pl.loop(0, 2)
        def _(tile):
            span = pl.ds(pl.multiple_of(tile * 2 * width, 2 * width), 2 * width)
            lhs = rows_of(every, half, unit)
            if kind == 0:
                part = jnp.dot(lhs, w_in[:, span], preferred_element_type=jnp.float32)
            else:
                part = lax.dot_general(
                    lhs, w_out[span, :], (((1,), (1,)), ((), ())),
                    preferred_element_type=jnp.float32,
                )
            part = b16(part)
            for piece in range(2):
                shard = (2 * tile + piece + SIDE - col) % SIDE
                cut = part[:, piece * width : (piece + 1) * width]
                mine[shard] = cut.reshape(SIZES[half][unit], HALF, width)

        sums[kind, half, unit] = [
            send(mine.at[2, high], fwd.at[0, high], ring_y.after),
            send(mine.at[2, low], fwd.at[1, low], ring_y.before),
            send(mine.at[1, low], back.at[0, low], ring_y.after),
            send(mine.at[3, high], back.at[1, high], ring_y.before),
        ]

    def y_relay(kind, half, unit):
        mine, fwd, back, low, high = y_buffers(kind, half, unit)
        copies = sums[kind, half, unit]
        copies[0].wait_recv()
        mine[1, high] = b16(f32(mine[1, high]) + f32(fwd[0, high]))
        copies.append(send(mine.at[1, high], back.at[0, high], ring_y.after))
        copies[1].wait_recv()
        mine[3, low] = b16(f32(mine[3, low]) + f32(fwd[1, low]))
        copies.append(send(mine.at[3, low], back.at[1, low], ring_y.before))

    def y_total(kind, half, unit):
        for copy in sums[kind, half, unit][2:]:
            copy.wait_recv()
        mine, _, back, _, _ = y_buffers(kind, half, unit)
        return f32(mine[0]) + f32(back[0]) + f32(back[1])

    own_columns = pl.ds(pl.multiple_of(col * width, width), width)

    def finish_hidden(half, unit):
        value, steep = gelu_parts(y_total(0, half, unit))
        value = b16(value)
        at = 0
        for plane, lo, hi in UNITS[half][unit]:
            span = pl.ds(lo, hi - lo)
            g_all[half, plane, span, :, own_columns] = value[at : at + hi - lo]
            slope[half, plane, span] = steep[at : at + hi - lo]
            at += hi - lo

    def finish_grad(half):
        for unit, pieces in enumerate(UNITS[half]):
            total = y_total(1, half, unit)
            at = 0
            for plane, lo, hi in pieces:
                for block in range(lo, hi):
                    part = b16(total[at] * slope[half, block, plane])
                    dh_all[half, plane, block, :, own_columns] = part
                    at += 1

    keep = []
    shared = []

    def share(src, dst):
        keep.append(local(src, dst))
        shared.append(send(src, dst, twin))

    def share_inputs(half):
        share(x_all.at[half], x_hbm.at[layer, half])
        for plane in range(SIDE):
            share(dy_all.at[half, plane], dy_two.at[layer, half, :, plane])

    def group_of(kind, half, group):
        first, size = GROUPS[group]
        return (g_all, dh_all)[kind].at[half, pl.ds(first, size)]

    def columns_of(step):
        at = (col + step + SIDE) % SIDE
        return pl.ds(pl.multiple_of(at * width, width), width)

    passes = {}

    def start(kind, half, group):
        own = group_of(kind, half, group).at[:, :, :, own_columns]
        passes[kind, half, group] = [send(own, own, ring_y.after), send(own, own, ring_y.before)]

    def relay(kind, half, group):
        copies, every = passes[kind, half, group], group_of(kind, half, group)
        copies[0].wait_recv()
        part = every.at[:, LO, :, columns_of(-1)]
        copies.append(send(part, part, ring_y.after))
        copies[1].wait_recv()
        part = every.at[:, HI, :, columns_of(1)]
        copies.append(send(part, part, ring_y.before))

    def product(kind, half, group):
        first, size = GROUPS[group]
        every = (g_all, dh_all)[kind]

        @pl.loop(0, 4)
        def _(tile):
            cols = w_out.shape[1] // 4
            span = pl.ds(pl.multiple_of(tile * cols, cols), cols)
            lhs = every[half, pl.ds(first, size)].reshape(-1, every.shape[-1])
            if kind == 0:
                part = jnp.dot(lhs, w_out[:, span], preferred_element_type=jnp.float32)
            else:
                part = lax.dot_general(
                    lhs, w_in[span, :], (((1,), (1,)), ((), ())),
                    preferred_element_type=jnp.float32,
                )
            part = part.reshape(size, SIDE, HALF, cols)
            if first == OWN:
                zown[kind, half, :, :, span] = part[0]
                part = part[1:]
            if size > 1:
                zsum[kind, half, pl.ds(1, 3), :, :, span] = b16(part)

    moves = {}
    plane_rings = (ring_z, ring_x)
    block_rings = (ring_x, ring_z)

    def planes_start(kind, half):
        ring = plane_rings[kind]
        mine, fwd, back = zsum.at[kind, half], zfwd.at[kind, half], zback.at[kind, half]
        moves[kind, half, FAR] = (
            send(mine.at[FAR, HI], fwd.at[0], ring.after),
            send(mine.at[FAR, LO], fwd.at[1], ring.before),
        )
        moves[kind, half, OWN] = [
            send(mine.at[NEXT, LO], back.at[0, LO], ring.after),
            send(mine.at[PREV, HI], back.at[1, HI], ring.before),
        ]

    def planes_relay(kind, half):
        ring = plane_rings[kind]
        mine, fwd, back = zsum.at[kind, half], zfwd.at[kind, half], zback.at[kind, half]
        moves[kind, half, FAR][0].wait_recv()
        mine[NEXT, HI] = b16(f32(mine[NEXT, HI]) + f32(fwd[0]))
        moves[kind, half, OWN].append(send(mine.at[NEXT, HI], back.at[0, HI], ring.after))
        moves[kind, half, FAR][1].wait_recv()
        mine[PREV, LO] = b16(f32(mine[PREV, LO]) + f32(fwd[1]))
        moves[kind, half, OWN].append(send(mine.at[PREV, LO], back.at[1, LO], ring.before))

    lasts = {}

    def blocks_start(kind, half):
        ring = block_rings[kind]
        for copy in moves[kind, half, OWN]:
            copy.wait_recv()
        own, others = zown.at[kind, half], zback.at[kind, half]
        mine, fwd, back = xsum.at[kind, half], xfwd.at[kind, half], xback.at[kind, half]
        for block in (FAR, NEXT, PREV, OWN):
            total = own[block] + f32(others[0, block]) + f32(others[1, block])
            if block == OWN:
                own[OWN] = total
            else:
                mine[block] = b16(total)
        lasts[kind, half] = [
            send(mine.at[FAR, :, right], fwd.at[0], ring.after),
            send(mine.at[FAR, :, left], fwd.at[1], ring.before),
            send(mine.at[NEXT, :, left], back.at[0, :, left], ring.after),
            send(mine.at[PREV, :, right], back.at[1, :, right], ring.before),
        ]

    def blocks_relay(kind, half):
        ring, copies = block_rings[kind], lasts[kind, half]
        mine, fwd, back = xsum.at[kind, half], xfwd.at[kind, half], xback.at[kind, half]
        copies[0].wait_recv()
        mine[NEXT, :, right] = b16(f32(mine[NEXT, :, right]) + f32(fwd[0]))
        copies.append(send(mine.at[NEXT, :, right], back.at[0, :, right], ring.after))
        copies[1].wait_recv()
        mine[PREV, :, left] = b16(f32(mine[PREV, :, left]) + f32(fwd[1]))
        copies.append(send(mine.at[PREV, :, left], back.at[1, :, left], ring.before))

    def blocks_total(kind, half):
        for copy in lasts[kind, half][2:]:
            copy.wait_recv()
        rows = pl.ds(half * HALF, HALF)
        own, back = zown.at[kind, half], xback.at[kind, half]
        total = f32((x_ref, dy_ref)[kind][rows]) + own[OWN] + f32(back[0]) + f32(back[1])
        (out_ref, grad_ref)[kind][rows] = b16(total)

    def finish(kind, half, group):
        for copy in passes[kind, half, group][2:]:
            copy.wait_recv()
        first, size = GROUPS[group]
        if kind == 0:
            span = pl.ds(first, size)
            share(g_all.at[half, span], g_two.at[layer, half, span])
        else:
            for plane in range(first, first + size):
                share(dh_all.at[half, plane], dh_hbm.at[layer, half, :, plane])
        product(kind, half, group)
        if size > 1:
            planes_start(kind, half)

    def settle():
        for copy in keep:
            copy.wait()
        for copy in shared:
            copy.wait_recv()
        keep.clear()
        shared.clear()

    def out_gradient(tile):
        rows = 512
        span = pl.ds(tile * rows, rows)

        @pl.loop(0, 2)
        def _(side):
            cols = dy_two.shape[-1] // 2
            part = pl.ds(pl.multiple_of(side * cols, cols), cols)
            lhs = g_two[:, :, :, :, :, span].reshape(-1, rows)
            rhs = dy_two[:, :, :, :, :, part].reshape(-1, cols)
            total = lax.dot_general(
                lhs, rhs, (((0,), (0,)), ((), ())), preferred_element_type=jnp.float32
            )
            w_out_grad[span, part] = b16(total)

        keep.append(local(w_out_grad.at[span], w_out_grad_hbm.at[span]))

    for kind in range(2):
        take_line(kind, 0)
    for kind in range(2):
        take_block(kind, 0, OWN)
    load_in.wait()
    y_product(0, 0, 0)
    for kind in range(2):
        take_line_far(kind, 0)
    load_out.wait()
    y_product(1, 0, 0)
    for kind in range(2):
        open_line(kind, 1)
        share_block(kind, 1, OWN)
    for kind in range(2):
        take_block(kind, 0, PREV)
        take_block(kind, 0, NEXT)
    y_relay(0, 0, 0)
    y_relay(1, 0, 0)
    for kind in range(2):
        take_block(kind, 0, FAR)
    for kind in range(2):
        take_line(kind, 1)
    for kind in range(2):
        take_far(kind, 0)
    y_product(0, 0, 1)
    y_product(1, 0, 1)
    finish_hidden(0, 0)
    for kind in range(2):
        take_block(kind, 1, OWN)
        take_line_far(kind, 1)
    y_relay(0, 0, 1)
    for kind in range(2):
        take_block(kind, 1, PREV)
        take_block(kind, 1, NEXT)
    y_relay(1, 0, 1)
    finish_hidden(0, 1)
    start(0, 0, "all")
    for kind in range(2):
        take_block(kind, 1, FAR)
    finish_grad(0)
    start(1, 0, "all")
    for kind in range(2):
        take_far(kind, 1)
    y_product(0, 1, 0)
    relay(0, 0, "all")
    y_product(1, 1, 0)
    relay(1, 0, "all")
    y_relay(0, 1, 0)
    finish(0, 0, "all")
    y_relay(1, 1, 0)
    finish(1, 0, "all")
    finish_hidden(1, 0)
    start(0, 1, "others")
    finish_grad(1)
    start(1, 1, "others")
    planes_relay(0, 0)
    planes_relay(1, 0)
    relay(0, 1, "others")
    start(0, 1, "own")
    relay(1, 1, "others")
    start(1, 1, "own")
    finish(0, 1, "others")
    relay(0, 1, "own")
    blocks_start(0, 0)
    finish(1, 1, "others")
    relay(1, 1, "own")
    blocks_start(1, 0)
    share_inputs(0)
    share_inputs(1)
    finish(0, 1, "own")
    planes_relay(0, 1)
    blocks_relay(0, 0)
    finish(1, 1, "own")
    planes_relay(1, 1)
    blocks_relay(1, 0)
    settle()
    out_gradient(0)
    blocks_start(0, 1)
    blocks_start(1, 1)
    blocks_total(0, 0)
    blocks_total(1, 0)
    out_gradient(1)
    blocks_relay(0, 1)
    blocks_relay(1, 1)
    out_gradient(2)
    blocks_total(0, 1)
    blocks_total(1, 1)

    for copy in keep:
        copy.wait()
    for copy in shared:
        copy.wait_recv()
    for wait_send in sent:
        wait_send()


def run_block(x, dy, w_in, w_out):
    tokens, features = x.shape
    hidden = w_in.shape[1]
    width = hidden // SIDE
    held = (2, SIDE, SIDE, HALF)
    bf, fl = jnp.bfloat16, jnp.float32
    vmem = pl.BlockSpec(memory_space=pltpu.VMEM)
    hbm = pl.BlockSpec(memory_space=pl.ANY)
    shape = jax.ShapeDtypeStruct
    return pl.pallas_call(
        block_kernel,
        out_shape=(
            shape((tokens, features), bf),
            shape((tokens, features), bf),
            shape((2,) + held + (features,), bf),
            shape((2,) + held + (hidden,), bf),
            shape(w_out.shape, bf),
        ),
        in_specs=[vmem, vmem, hbm, hbm],
        out_specs=(vmem, vmem, hbm, hbm, hbm),
        scratch_shapes=[
            pltpu.VMEM(w_in.shape, bf),
            pltpu.VMEM(w_out.shape, bf),
            pltpu.VMEM(held + (features,), bf),
            pltpu.VMEM(held + (features,), bf),
            pltpu.VMEM(held + (hidden,), bf),
            pltpu.VMEM(held + (hidden,), bf),
            pltpu.VMEM(held + (width,), fl),
            pltpu.VMEM((2,) + held + (hidden,), bf),
            pltpu.VMEM((2,) + held + (features,), bf),
            pltpu.VMEM(w_out.shape, bf),
            pltpu.VMEM((2, 2, SIDE, 16, HALF, width), bf),
            pltpu.VMEM((2, 2, 2, 16, HALF, width), bf),
            pltpu.VMEM((2, 2, 2, 16, HALF, width), bf),
            pltpu.VMEM((2, 2, SIDE, SIDE, HALF, features), bf),
            pltpu.VMEM((2, 2, 2, 2, HALF, features), bf),
            pltpu.VMEM((2, 2, 2, SIDE, HALF, features), bf),
            pltpu.VMEM((2, 2, SIDE, HALF, features), fl),
            pltpu.VMEM((2, 2, SIDE, HALF, features), bf),
            pltpu.VMEM((2, 2, 2, HALF, features // 2), bf),
            pltpu.VMEM((2, 2, 2, HALF, features), bf),
            pltpu.SemaphoreType.DMA((N_SEMS,)),
        ],
        compiler_params=pltpu.CompilerParams(
            collective_id=1, has_side_effects=True, vmem_limit_bytes=60 * 2**20
        ),
    )(x, dy, w_in, w_out)


def grads_kernel(x_ref, dh_ref, kept_ref, out_ref, grad_ref, w_in_grad, w_out_grad, out, grad):
    part = lax.dot_general(
        x_ref[...], dh_ref[...], (((0,), (0,)), ((), ())), preferred_element_type=jnp.float32
    )
    w_in_grad[...] = b16(part)
    w_out_grad[...] = kept_ref[...]

    @pl.when(pl.program_id(0) == 0)
    def _():
        out[...] = out_ref[...]
        grad[...] = grad_ref[...]


def per_device(layer_input, w_in, w_out, output_grad):
    out, grad, x_two, dh_two, kept = run_block(layer_input, output_grad, w_in, w_out)
    features, hidden = w_in.shape
    x_two, dh_two = x_two.reshape(-1, features), dh_two.reshape(-1, hidden)
    tokens, steps = x_two.shape[0], 4
    small = pl.BlockSpec(out.shape, lambda i: (0, 0))
    wide = pl.BlockSpec((features // steps, hidden), lambda i: (i, 0))
    tall = pl.BlockSpec((hidden // steps, features), lambda i: (i, 0))
    bf = jnp.bfloat16
    w_in_grad, w_out_grad, out, grad = pl.pallas_call(
        grads_kernel,
        grid=(steps,),
        out_shape=[jax.ShapeDtypeStruct(a.shape, bf) for a in (w_in, w_out, out, grad)],
        in_specs=[
            pl.BlockSpec((tokens, features // steps), lambda i: (0, i)),
            pl.BlockSpec((tokens, hidden), lambda i: (0, 0)),
            tall,
            small,
            small,
        ],
        out_specs=[wide, tall, small, small],
        compiler_params=pltpu.CompilerParams(vmem_limit_bytes=60 * 2**20),
    )(x_two, dh_two, kept, out, grad)
    return (out, grad, w_in_grad, w_out_grad)


def solution(mesh):
    in_specs = (
        P(("depth", "row"), "col"),
        P("col", "row"),
        P("row", "col"),
        P(("depth", "row"), "col"),
    )
    out_specs = (
        P(("depth", "row"), "col"),
        P(("depth", "row"), "col"),
        P("col", "row"),
        P("row", "col"),
    )
    return jax.shard_map(
        per_device, mesh=mesh, in_specs=in_specs, out_specs=out_specs, check_vma=False
    )
```

time: 487 us -> 118 us (0.24)
  waiting for transfers between devices: 402 us -> 0 us
  Pallas kernels: 0 us -> 117 us
  matrix products: 48 us -> 0 us
  local copies, waits for them, and re-layouts: 15.2 us -> 0 us
  between operations: 13.9 us -> 0.8 us
  other arithmetic: 6.04 us -> 0 us
    reduce_scatter x4 -> x0, waiting for transfers between devices: 211 us -> none  [the longest x1 79.2 us: per_device(): lax.psum_scatter(contract_last(rows, w_in), 'row', scatter_dimension=0, t...]
    all_gather x4 -> x0, waiting for transfers between devices: 133 us -> none  [the longest x1 49.2 us: per_device(): lax.all_gather(output_grad, 'row', axis=0, tiled=True)]
    pallas_call x0 -> x2, Pallas kernels: none -> 117 us  [the longest x1 103 us: run_block(): pl.pallas_call(block_kernel, out_shape=(shape((tokens, features), bf), sh...]
    psum x1 -> x0, waiting for transfers between devices: 55.9 us -> none  [per_device(): lax.psum(part_in.astype(jnp.bfloat16), 'depth').astype(jnp.float32)]
    dot_general x6 -> x0, matrix products: 48 us -> none  [the longest x2 17.2 us: contract_last(): lax.dot_general(left, right, (((1,), (1,)), ((), ())), preferred_element_...]
    unnamed x10 -> x0, local copies, waits for them, and re-layouts: 15.2 us -> none
    convert_element_type x3 -> x0, other arithmetic: 6.04 us -> none  [the longest x1 2.78 us: per_device(): grad_hid = (grad_act * slope).astype(jnp.bfloat16)]
  transfers between devices with their start and end apart: 9 -> 0, of which waited for: 9 -> 0; matrix products, arithmetic and copies ran while one was open for 11% -> 0% of each run, Pallas kernels for 0% -> 0%
where the time goes in v2:
time: 118 us
  Pallas kernels  117 us (99%)
    pallas_call x1, Pallas kernels, run_block(): pl.pallas_call(block_kernel, out_shape=(shape((tokens, features), bf), sh...  103 us
    pallas_call x1, Pallas kernels, per_device(): pl.pallas_call(grads_kernel, grid=(steps,), out_shape=[jax.ShapeDtypeStru...  13.4 us

profile of v2, /device:TPU:0, one launch (start us, length us, event | category | flops | bytes accessed | tf_op | source)
XLA Modules:
  0.0 117.6 jit_solution(15411678300293496119)
XLA Ops:
  0.6 103.4 %shard_map.75 = (bf16[32,2048]{1,0:T(8,128)(2,1)}, bf16[32,2048]{1,0:T(8,128)(2,1)}, bf16[2,2,4,4,16,2048]{5,4,3,2,1,0:T(8,128)(2,1)}, bf16[2,2,4,4,16,1536]{5,4,3,2,1,0:T(8,128)(2,1)}, bf16[1536,2048]{1,0:T(8,128)(2,1)}) custom-call(bf16[32,2048]{1,0:T(8,128)(2,1)} %x_ref.1, bf16[32,2048]{1,0:T(8,128)(2,1)} %dy_ref.1, bf16[2048,1536]{1,0:T(8,128)(2,1)} %w_in_hbm.1, ...), custom_call_target="tpu_custom_call" | custom-call | tf_op jit(solution)/shard_map/pallas_call | solution.py:511
  104.0 13.4 %shard_map.76 = (bf16[2048,1536]{1,0:T(8,128)(2,1)}, bf16[1536,2048]{1,0:T(8,128)(2,1)}, bf16[32,2048]{1,0:T(8,128)(2,1)}, bf16[32,2048]{1,0:T(8,128)(2,1)}) custom-call(bf16[1024,2048]{1,0:T(8,128)(2,1)} %bitcast.2, bf16[1024,1536]{1,0:T(8,128)(2,1)} %bitcast.3, bf16[1536,2048]{1,0:T(8,128)(2,1)} %get-tuple-element.15.kept_ref, ...), custom_call_target="tpu_custom_call" | custom-call | tf_op jit(solution)/shard_map/pallas_call | solution.py:573

commit v3 on v2

--- a/solution.py
+++ b/solution.py
@@ -21,7 +21,8 @@
 STARTS = tuple(tuple(sum(sizes[:unit]) for unit in range(len(sizes))) for sizes in SIZES)
 HALF = 16
 LO, HI = pl.ds(0, 2), pl.ds(2, 2)
-GROUPS = {"all": (OWN, 4), "others": (PREV, 3), "own": (OWN, 1)}
+BOTH = 2
+GROUPS = {"others": (PREV, 3), "own": (OWN, 1)}
 N_SEMS = 560
 
 
@@ -255,7 +256,10 @@
 
     def group_of(kind, half, group):
         first, size = GROUPS[group]
-        return (g_all, dh_all)[kind].at[half, pl.ds(first, size)]
+        every = (g_all, dh_all)[kind]
+        if half == BOTH:
+            return every.at[:, first]
+        return every.at[half, pl.ds(first, size)]
 
     def columns_of(step):
         at = (col + step + SIDE) % SIDE
@@ -284,7 +288,8 @@
         def _(tile):
             cols = w_out.shape[1] // 4
             span = pl.ds(pl.multiple_of(tile * cols, cols), cols)
-            lhs = every[half, pl.ds(first, size)].reshape(-1, every.shape[-1])
+            lhs = every[:, first] if half == BOTH else every[half, pl.ds(first, size)]
+            lhs = lhs.reshape(-1, every.shape[-1])
             if kind == 0:
                 part = jnp.dot(lhs, w_out[:, span], preferred_element_type=jnp.float32)
             else:
@@ -292,12 +297,11 @@
                     lhs, w_in[span, :], (((1,), (1,)), ((), ())),
                     preferred_element_type=jnp.float32,
                 )
-            part = part.reshape(size, SIDE, HALF, cols)
-            if first == OWN:
-                zown[kind, half, :, :, span] = part[0]
-                part = part[1:]
-            if size > 1:
-                zsum[kind, half, pl.ds(1, 3), :, :, span] = b16(part)
+            part = part.reshape(-1, SIDE, HALF, cols)
+            if half == BOTH:
+                zown[kind, :, :, :, span] = part
+            else:
+                zsum[kind, half, pl.ds(first, size), :, :, span] = b16(part)
 
     moves = {}
     plane_rings = (ring_z, ring_x)
@@ -368,14 +372,15 @@
         for copy in passes[kind, half, group][2:]:
             copy.wait_recv()
         first, size = GROUPS[group]
-        if kind == 0:
-            span = pl.ds(first, size)
-            share(g_all.at[half, span], g_two.at[layer, half, span])
-        else:
-            for plane in range(first, first + size):
-                share(dh_all.at[half, plane], dh_hbm.at[layer, half, :, plane])
+        for each in range(2) if half == BOTH else (half,):
+            if kind == 0:
+                span = pl.ds(first, size)
+                share(g_all.at[each, span], g_two.at[layer, each, span])
+            else:
+                for plane in range(first, first + size):
+                    share(dh_all.at[each, plane], dh_hbm.at[layer, each, :, plane])
         product(kind, half, group)
-        if size > 1:
+        if half != BOTH:
             planes_start(kind, half)
 
     def settle():
@@ -403,92 +408,96 @@
 
         keep.append(local(w_out_grad.at[span], w_out_grad_hbm.at[span]))
 
-    for kind in range(2):
-        take_line(kind, 0)
-    for kind in range(2):
-        take_block(kind, 0, OWN)
+    take_line(0, 0)
     load_in.wait()
+    take_line(1, 0)
+    take_line_far(0, 0)
+    take_block(1, 0, OWN)
+    take_block(0, 0, OWN)
     y_product(0, 0, 0)
-    for kind in range(2):
-        take_line_far(kind, 0)
+    take_block(0, 0, NEXT)
     load_out.wait()
+    open_line(0, 1)
+    take_line_far(1, 0)
+    take_block(0, 0, FAR)
+    take_block(0, 0, PREV)
+    y_relay(0, 0, 0)
+    take_block(1, 0, NEXT)
+    take_block(1, 0, PREV)
     y_product(1, 0, 0)
-    for kind in range(2):
-        open_line(kind, 1)
-        share_block(kind, 1, OWN)
-    for kind in range(2):
-        take_block(kind, 0, PREV)
-        take_block(kind, 0, NEXT)
-    y_relay(0, 0, 0)
+    open_line(1, 1)
+    take_block(1, 0, FAR)
+    share_block(0, 1, OWN)
+    take_far(0, 0)
+    y_product(0, 0, 1)
+    take_far(1, 0)
+    take_line(0, 1)
+    y_product(1, 0, 1)
+    take_line_far(0, 1)
+    y_relay(0, 0, 1)
+    take_line(1, 1)
+    finish_hidden(0, 0)
+    take_block(0, 1, FAR)
+    share_block(1, 1, OWN)
     y_relay(1, 0, 0)
-    for kind in range(2):
-        take_block(kind, 0, FAR)
-    for kind in range(2):
-        take_line(kind, 1)
-    for kind in range(2):
-        take_far(kind, 0)
-    y_product(0, 0, 1)
-    y_product(1, 0, 1)
-    finish_hidden(0, 0)
-    for kind in range(2):
-        take_block(kind, 1, OWN)
-        take_line_far(kind, 1)
-    y_relay(0, 0, 1)
-    for kind in range(2):
-        take_block(kind, 1, PREV)
-        take_block(kind, 1, NEXT)
     y_relay(1, 0, 1)
+    take_block(0, 1, PREV)
+    take_block(0, 1, OWN)
+    take_block(0, 1, NEXT)
     finish_hidden(0, 1)
-    start(0, 0, "all")
-    for kind in range(2):
-        take_block(kind, 1, FAR)
+    start(0, 0, "others")
+    take_line_far(1, 1)
     finish_grad(0)
-    start(1, 0, "all")
-    for kind in range(2):
-        take_far(kind, 1)
+    start(1, 0, "others")
+    take_far(0, 1)
+    take_block(1, 1, PREV)
+    take_block(1, 1, NEXT)
+    take_block(1, 1, FAR)
     y_product(0, 1, 0)
-    relay(0, 0, "all")
+    relay(0, 0, "others")
+    take_block(1, 1, OWN)
+    take_far(1, 1)
     y_product(1, 1, 0)
-    relay(1, 0, "all")
     y_relay(0, 1, 0)
-    finish(0, 0, "all")
+    finish(0, 0, "others")
+    share_inputs(1)
+    relay(1, 0, "others")
     y_relay(1, 1, 0)
-    finish(1, 0, "all")
     finish_hidden(1, 0)
     start(0, 1, "others")
     finish_grad(1)
     start(1, 1, "others")
+    finish(1, 0, "others")
+    relay(0, 1, "others")
+    relay(1, 1, "others")
     planes_relay(0, 0)
+    share_inputs(0)
+    start(1, BOTH, "own")
+    finish(0, 1, "others")
     planes_relay(1, 0)
-    relay(0, 1, "others")
-    start(0, 1, "own")
-    relay(1, 1, "others")
-    start(1, 1, "own")
-    finish(0, 1, "others")
-    relay(0, 1, "own")
+    start(0, BOTH, "own")
+    finish(1, 1, "others")
+    relay(1, BOTH, "own")
+    relay(0, BOTH, "own")
+    planes_relay(0, 1)
+    finish(1, BOTH, "own")
+    blocks_start(1, 0)
+    planes_relay(1, 1)
+    finish(0, BOTH, "own")
+    settle()
+    blocks_start(0, 1)
+    out_gradient(1)
     blocks_start(0, 0)
-    finish(1, 1, "others")
-    relay(1, 1, "own")
-    blocks_start(1, 0)
-    share_inputs(0)
-    share_inputs(1)
-    finish(0, 1, "own")
-    planes_relay(0, 1)
+    blocks_start(1, 1)
+    blocks_relay(0, 1)
+    out_gradient(2)
+    blocks_relay(1, 0)
     blocks_relay(0, 0)
-    finish(1, 1, "own")
-    planes_relay(1, 1)
-    blocks_relay(1, 0)
-    settle()
+    blocks_relay(1, 1)
     out_gradient(0)
-    blocks_start(0, 1)
-    blocks_start(1, 1)
+    blocks_total(1, 0)
+    blocks_total(0, 1)
     blocks_total(0, 0)
-    blocks_total(1, 0)
-    out_gradient(1)
-    blocks_relay(0, 1)
-    blocks_relay(1, 1)
-    out_gradient(2)
-    blocks_total(0, 1)
     blocks_total(1, 1)
 
     for copy in keep:

time: 118 us -> 114 us (0.966)
  Pallas kernels: 117 us -> 113 us
    pallas_call x1, Pallas kernels: 103 us -> 99.7 us  [run_block(): pl.pallas_call(block_kernel, out_shape=(shape((tokens, features), bf), sh...]
where the time goes in v3:
time: 114 us
  Pallas kernels  113 us (99%)
    pallas_call x1, Pallas kernels, run_block(): pl.pallas_call(block_kernel, out_shape=(shape((tokens, features), bf), sh...  99.7 us
    pallas_call x1, Pallas kernels, per_device(): pl.pallas_call(grads_kernel, grid=(steps,), out_shape=[jax.ShapeDtypeStru...  13.4 us

profile of v3, /device:TPU:0, one launch (start us, length us, event | category | flops | bytes accessed | tf_op | source)
XLA Modules:
  0.0 113.9 jit_solution(13848464890390818441)
XLA Ops:
  0.6 99.7 %shard_map.75 = (bf16[32,2048]{1,0:T(8,128)(2,1)}, bf16[32,2048]{1,0:T(8,128)(2,1)}, bf16[2,2,4,4,16,2048]{5,4,3,2,1,0:T(8,128)(2,1)}, bf16[2,2,4,4,16,1536]{5,4,3,2,1,0:T(8,128)(2,1)}, bf16[1536,2048]{1,0:T(8,128)(2,1)}) custom-call(bf16[32,2048]{1,0:T(8,128)(2,1)} %x_ref.1, bf16[32,2048]{1,0:T(8,128)(2,1)} %dy_ref.1, bf16[2048,1536]{1,0:T(8,128)(2,1)} %w_in_hbm.1, ...), custom_call_target="tpu_custom_call" | custom-call | tf_op jit(solution)/shard_map/pallas_call | solution.py:520
  100.3 13.4 %shard_map.76 = (bf16[2048,1536]{1,0:T(8,128)(2,1)}, bf16[1536,2048]{1,0:T(8,128)(2,1)}, bf16[32,2048]{1,0:T(8,128)(2,1)}, bf16[32,2048]{1,0:T(8,128)(2,1)}) custom-call(bf16[1024,2048]{1,0:T(8,128)(2,1)} %bitcast.2, bf16[1024,1536]{1,0:T(8,128)(2,1)} %bitcast.3, bf16[1536,2048]{1,0:T(8,128)(2,1)} %get-tuple-element.15.kept_ref, ...), custom_call_target="tpu_custom_call" | custom-call | tf_op jit(solution)/shard_map/pallas_call | solution.py:582

commit v4 on v3

--- a/solution.py
+++ b/solution.py
@@ -13,7 +13,8 @@
 UNITS = (
     (
         ((OWN, 0, 3), (PREV, 0, 1), (NEXT, 0, 1)),
-        ((OWN, 3, 4), (PREV, 1, 4), (NEXT, 1, 4), (FAR, 0, 4)),
+        ((PREV, 1, 3), (NEXT, 1, 3)),
+        ((OWN, 3, 4), (PREV, 3, 4), (NEXT, 3, 4), (FAR, 0, 4)),
     ),
     (((OWN, 0, 4), (PREV, 0, 4), (NEXT, 0, 4), (FAR, 0, 4)),),
 )
@@ -180,7 +181,7 @@
         mine, fwd, back, low, high = y_buffers(kind, half, unit)
         every = (x_all, dy_all)[kind]
 
-        @pl.loop(0, 2)
+        @pl.loop(0, 2, unroll=True)
         def _(tile):
             span = pl.ds(pl.multiple_of(tile * 2 * width, 2 * width), 2 * width)
             lhs = rows_of(every, half, unit)
@@ -284,7 +285,7 @@
         first, size = GROUPS[group]
         every = (g_all, dh_all)[kind]
 
-        @pl.loop(0, 4)
+        @pl.loop(0, 4, unroll=True)
         def _(tile):
             cols = w_out.shape[1] // 4
             span = pl.ds(pl.multiple_of(tile * cols, cols), cols)
@@ -300,6 +301,8 @@
             part = part.reshape(-1, SIDE, HALF, cols)
             if half == BOTH:
                 zown[kind, :, :, :, span] = part
+            elif first == OWN:
+                zown[kind, half, :, :, span] = part[0]
             else:
                 zsum[kind, half, pl.ds(first, size), :, :, span] = b16(part)
 
@@ -380,7 +383,7 @@
                 for plane in range(first, first + size):
                     share(dh_all.at[each, plane], dh_hbm.at[layer, each, :, plane])
         product(kind, half, group)
-        if half != BOTH:
+        if first != OWN:
             planes_start(kind, half)
 
     def settle():
@@ -409,95 +412,106 @@
         keep.append(local(w_out_grad.at[span], w_out_grad_hbm.at[span]))
 
     take_line(0, 0)
+    take_line_far(0, 0)
     load_in.wait()
+    open_line(0, 1)
     take_line(1, 0)
-    take_line_far(0, 0)
+    load_out.wait()
     take_block(1, 0, OWN)
+    y_product(1, 0, 0)
+    take_block(0, 0, PREV)
     take_block(0, 0, OWN)
+    take_block(0, 0, NEXT)
     y_product(0, 0, 0)
-    take_block(0, 0, NEXT)
-    load_out.wait()
-    open_line(0, 1)
+    take_block(0, 0, FAR)
     take_line_far(1, 0)
-    take_block(0, 0, FAR)
-    take_block(0, 0, PREV)
+    y_product(0, 0, 1)
+    take_line(0, 1)
+    y_relay(1, 0, 0)
     y_relay(0, 0, 0)
     take_block(1, 0, NEXT)
+    take_far(0, 0)
+    y_product(0, 0, 2)
     take_block(1, 0, PREV)
-    y_product(1, 0, 0)
-    open_line(1, 1)
     take_block(1, 0, FAR)
     share_block(0, 1, OWN)
-    take_far(0, 0)
-    y_product(0, 0, 1)
-    take_far(1, 0)
-    take_line(0, 1)
+    open_line(1, 1)
     y_product(1, 0, 1)
     take_line_far(0, 1)
     y_relay(0, 0, 1)
+    share_block(1, 1, OWN)
+    y_relay(0, 0, 2)
+    take_far(1, 0)
+    y_product(1, 0, 2)
     take_line(1, 1)
+    take_block(0, 1, PREV)
+    finish_hidden(0, 1)
+    take_block(0, 1, FAR)
+    y_relay(1, 0, 1)
     finish_hidden(0, 0)
-    take_block(0, 1, FAR)
-    share_block(1, 1, OWN)
-    y_relay(1, 0, 0)
-    y_relay(1, 0, 1)
-    take_block(0, 1, PREV)
+    finish_hidden(0, 2)
+    start(0, 0, "own")
+    take_block(0, 1, NEXT)
     take_block(0, 1, OWN)
-    take_block(0, 1, NEXT)
-    finish_hidden(0, 1)
     start(0, 0, "others")
+    take_block(1, 1, PREV)
+    take_far(0, 1)
     take_line_far(1, 1)
+    y_relay(1, 0, 2)
+    relay(0, 0, "own")
+    y_product(0, 1, 0)
+    take_block(1, 1, NEXT)
+    take_block(1, 1, OWN)
+    share_inputs(0)
+    relay(0, 0, "others")
     finish_grad(0)
     start(1, 0, "others")
-    take_far(0, 1)
-    take_block(1, 1, PREV)
-    take_block(1, 1, NEXT)
     take_block(1, 1, FAR)
-    y_product(0, 1, 0)
-    relay(0, 0, "others")
-    take_block(1, 1, OWN)
     take_far(1, 1)
     y_product(1, 1, 0)
     y_relay(0, 1, 0)
     finish(0, 0, "others")
-    share_inputs(1)
     relay(1, 0, "others")
     y_relay(1, 1, 0)
     finish_hidden(1, 0)
     start(0, 1, "others")
+    finish(1, 0, "others")
+    start(0, 1, "own")
     finish_grad(1)
     start(1, 1, "others")
-    finish(1, 0, "others")
+    planes_relay(0, 0)
+    finish(0, 0, "own")
     relay(0, 1, "others")
+    share_inputs(1)
+    blocks_start(0, 0)
+    planes_relay(1, 0)
+    start(1, 0, "own")
     relay(1, 1, "others")
-    planes_relay(0, 0)
-    share_inputs(0)
-    start(1, BOTH, "own")
     finish(0, 1, "others")
-    planes_relay(1, 0)
-    start(0, BOTH, "own")
+    relay(0, 1, "own")
+    relay(1, 0, "own")
+    start(1, 1, "own")
+    blocks_relay(0, 0)
     finish(1, 1, "others")
-    relay(1, BOTH, "own")
-    relay(0, BOTH, "own")
+    finish(1, 0, "own")
+    blocks_start(1, 0)
+    relay(1, 1, "own")
+    finish(0, 1, "own")
     planes_relay(0, 1)
-    finish(1, BOTH, "own")
-    blocks_start(1, 0)
+    settle()
     planes_relay(1, 1)
-    finish(0, BOTH, "own")
-    settle()
+    blocks_total(0, 0)
+    out_gradient(0)
+    finish(1, 1, "own")
+    blocks_relay(1, 0)
     blocks_start(0, 1)
+    blocks_start(1, 1)
     out_gradient(1)
-    blocks_start(0, 0)
-    blocks_start(1, 1)
     blocks_relay(0, 1)
+    blocks_relay(1, 1)
     out_gradient(2)
-    blocks_relay(1, 0)
-    blocks_relay(0, 0)
-    blocks_relay(1, 1)
-    out_gradient(0)
     blocks_total(1, 0)
     blocks_total(0, 1)
-    blocks_total(0, 0)
     blocks_total(1, 1)
 
     for copy in keep:

time: 114 us -> 112 us (0.982)
  Pallas kernels: 113 us -> 111 us
    pallas_call x1, Pallas kernels: 99.7 us -> 97.3 us  [run_block(): pl.pallas_call(block_kernel, out_shape=(shape((tokens, features), bf), sh...]
where the time goes in v4:
time: 112 us
  Pallas kernels  111 us (99%)
    pallas_call x1, Pallas kernels, run_block(): pl.pallas_call(block_kernel, out_shape=(shape((tokens, features), bf), sh...  97.3 us
    pallas_call x1, Pallas kernels, per_device(): pl.pallas_call(grads_kernel, grid=(steps,), out_shape=[jax.ShapeDtypeStru...  13.4 us

profile of v4, /device:TPU:0, one launch (start us, length us, event | category | flops | bytes accessed | tf_op | source)
XLA Modules:
  0.0 111.5 jit_solution(1804361892037499843)
XLA Ops:
  0.6 97.3 %shard_map.75 = (bf16[32,2048]{1,0:T(8,128)(2,1)}, bf16[32,2048]{1,0:T(8,128)(2,1)}, bf16[2,2,4,4,16,2048]{5,4,3,2,1,0:T(8,128)(2,1)}, bf16[2,2,4,4,16,1536]{5,4,3,2,1,0:T(8,128)(2,1)}, bf16[1536,2048]{1,0:T(8,128)(2,1)}) custom-call(bf16[32,2048]{1,0:T(8,128)(2,1)} %x_ref.1, bf16[32,2048]{1,0:T(8,128)(2,1)} %dy_ref.1, bf16[2048,1536]{1,0:T(8,128)(2,1)} %w_in_hbm.1, ...), custom_call_target="tpu_custom_call" | custom-call | tf_op jit(solution)/shard_map/pallas_call | solution.py:534
  98.0 13.4 %shard_map.76 = (bf16[2048,1536]{1,0:T(8,128)(2,1)}, bf16[1536,2048]{1,0:T(8,128)(2,1)}, bf16[32,2048]{1,0:T(8,128)(2,1)}, bf16[32,2048]{1,0:T(8,128)(2,1)}) custom-call(bf16[1024,2048]{1,0:T(8,128)(2,1)} %bitcast.2, bf16[1024,1536]{1,0:T(8,128)(2,1)} %bitcast.3, bf16[1536,2048]{1,0:T(8,128)(2,1)} %get-tuple-element.15.kept_ref, ...), custom_call_target="tpu_custom_call" | custom-call | tf_op jit(solution)/shard_map/pallas_call | solution.py:596

commit v5 on v4

--- a/solution.py
+++ b/solution.py
@@ -53,7 +53,7 @@
 
 
 def block_kernel(
-    x_ref, dy_ref, w_in_hbm, w_out_hbm,
+    x_hbm_in, dy_hbm_in, w_in_hbm, w_out_hbm,
     out_ref, grad_ref, x_hbm, dh_hbm, w_out_grad_hbm,
     w_in, w_out, x_all, dy_all, g_all, dh_all, slope, g_two, dy_two, w_out_grad,
     ysum, yfwd, yback, zsum, zfwd, zback, zown, xsum, xfwd, xback,
@@ -93,6 +93,11 @@
         copy.start()
         return copy
 
+    own = []
+    for half in range(2):
+        rows = pl.ds(half * HALF, HALF)
+        own.append(local(x_hbm_in.at[rows], x_all.at[half, OWN, OWN]))
+        own.append(local(dy_hbm_in.at[rows], dy_all.at[half, OWN, OWN]))
     load_in = local(w_in_hbm, w_in)
     load_out = local(w_out_hbm, w_out)
 
@@ -101,10 +106,8 @@
     greeted += (ring_y.after, ring_y.before, twin)
     for other in greeted:
         pl.semaphore_signal(barrier, inc=1, device_id=other, device_id_type=MESH)
-    for half in range(2):
-        rows = pl.ds(half * HALF, HALF)
-        x_all[half, OWN, OWN] = x_ref[rows]
-        dy_all[half, OWN, OWN] = dy_ref[rows]
+    for copy in own:
+        copy.wait()
     pl.semaphore_wait(barrier, len(greeted))
 
     kinds = ((x_all, ring_x, ring_z), (dy_all, ring_z, ring_x))
@@ -285,9 +288,9 @@
         first, size = GROUPS[group]
         every = (g_all, dh_all)[kind]
 
-        @pl.loop(0, 4, unroll=True)
+        @pl.loop(0, 2, unroll=True)
         def _(tile):
-            cols = w_out.shape[1] // 4
+            cols = w_out.shape[1] // 2
             span = pl.ds(pl.multiple_of(tile * cols, cols), cols)
             lhs = every[:, first] if half == BOTH else every[half, pl.ds(first, size)]
             lhs = lhs.reshape(-1, every.shape[-1])
@@ -368,7 +371,7 @@
             copy.wait_recv()
         rows = pl.ds(half * HALF, HALF)
         own, back = zown.at[kind, half], xback.at[kind, half]
-        total = f32((x_ref, dy_ref)[kind][rows]) + own[OWN] + f32(back[0]) + f32(back[1])
+        total = f32((x_all, dy_all)[kind][half, OWN, OWN]) + own[OWN] + f32(back[0]) + f32(back[1])
         (out_ref, grad_ref)[kind][rows] = b16(total)
 
     def finish(kind, half, group):
@@ -540,7 +543,7 @@
             shape((2,) + held + (hidden,), bf),
             shape(w_out.shape, bf),
         ),
-        in_specs=[vmem, vmem, hbm, hbm],
+        in_specs=[hbm, hbm, hbm, hbm],
         out_specs=(vmem, vmem, hbm, hbm, hbm),
         scratch_shapes=[
             pltpu.VMEM(w_in.shape, bf),

time: 112 us -> 111 us (level)
  no operation moved by 1% of the time
where the time goes in v5:
time: 111 us
  Pallas kernels  110 us (99%)
    pallas_call x1, Pallas kernels, run_block(): pl.pallas_call(block_kernel, out_shape=(shape((tokens, features), bf), sh...  96.4 us
    pallas_call x1, Pallas kernels, per_device(): pl.pallas_call(grads_kernel, grid=(steps,), out_shape=[jax.ShapeDtypeStru...  13.4 us

profile of v5, /device:TPU:0, one launch (start us, length us, event | category | flops | bytes accessed | tf_op | source)
XLA Modules:
  0.0 110.6 jit_solution(10597716383338147811)
XLA Ops:
  0.6 96.4 %shard_map.75 = (bf16[32,2048]{1,0:T(8,128)(2,1)}, bf16[32,2048]{1,0:T(8,128)(2,1)}, bf16[2,2,4,4,16,2048]{5,4,3,2,1,0:T(8,128)(2,1)}, bf16[2,2,4,4,16,1536]{5,4,3,2,1,0:T(8,128)(2,1)}, bf16[1536,2048]{1,0:T(8,128)(2,1)}) custom-call(bf16[32,2048]{1,0:T(8,128)(2,1)} %x_hbm_in.1, bf16[32,2048]{1,0:T(8,128)(2,1)} %dy_hbm_in.1, bf16[2048,1536]{1,0:T(8,128)(2,1)} %w_in_hbm.1, ...), custom_call_target="tpu_custom_call" | custom-call | tf_op jit(solution)/shard_map/pallas_call | solution.py:537
  97.1 13.4 %shard_map.76 = (bf16[2048,1536]{1,0:T(8,128)(2,1)}, bf16[1536,2048]{1,0:T(8,128)(2,1)}, bf16[32,2048]{1,0:T(8,128)(2,1)}, bf16[32,2048]{1,0:T(8,128)(2,1)}) custom-call(bf16[1024,2048]{1,0:T(8,128)(2,1)} %bitcast.2, bf16[1024,1536]{1,0:T(8,128)(2,1)} %bitcast.3, bf16[1536,2048]{1,0:T(8,128)(2,1)} %get-tuple-element.15.kept_ref, ...), custom_call_target="tpu_custom_call" | custom-call | tf_op jit(solution)/shard_map/pallas_call | solution.py:599
